TPU v7x, 32 devices: a whole 2x2x4 slice. The times are simulated.
32 devices in a mesh: section: 4 (over y, x), dp: 8 (over z, core).
Axes of the slice: x: 2, y: 2, z: 4, core: 2. Of those that a mesh axis runs over, the one named last changes fastest.
Arguments:
- section_inputs: bfloat16 [4, 1024, 4096], P('section', 'dp'), may hold values from -6 to 6
- gains: float32 [4, 4096], P('section'), may hold values from 0.25 to 1.75
- value_weight: bfloat16 [4, 4096, 1024], P('section', 'dp'), may hold values from -0.09375 to 0.09375
- top_cotangent: bfloat16 [1024, 4096], P('dp'), may hold values from -6 to 6
- proxy_loss: float32 [1024], P('dp'), may hold values from 0.5 to 5.5
- reference_loss: float32 [1024], P('dp'), may hold values from 1 to 3
- lengths: int32 [8, 8], P('dp'), may hold values from 1 to 80, 128 in all within a row
- doc_domain: int32 [8, 8], P('dp'), may hold values from 0 to 21
- log_weights: float32 [22], replicated, may hold values from -4 to -1
- step_count: int32 [1], replicated, may hold values from 1 to 256
Outputs:
- section_grads: bfloat16 [4, 1024, 4096], P('section', 'dp')
- weight_grads: float32 [4, 4096, 1024], P('section', 'dp')
- new_log_weights: float32 [22], replicated
Inputs may be any that keep to these rules, and one draw needn't show every extreme that they name: `lengths`: each row sums to 128: the documents fill their pack in order.
All inputs are finite; a program needn't handle non-finite values.
Results may differ from a plain program's by a relative error of at most 0.0071.
Values may be sent and summed in bfloat16 or wider, within the bound.
A program may use at most 128 MiB of HBM per device.

v0:
```python
import jax
import jax.numpy as jnp
from jax import lax
from jax.sharding import PartitionSpec as P

D = 4096
KV = 1024
DOMAINS = 22
MICRO = 4
DOCS = 8


EPS = 1e-05
SMOOTH = 0.001


def passed_along(shard, axis, by):
    size = lax.axis_size(axis)
    pairs = [(i, i + by) for i in range(size) if 0 <= i + by < size]
    return lax.ppermute(shard, axis, pairs)


def local_statistics(proxy_loss, reference_loss, lengths, doc_domain):
    rows = proxy_loss.shape[0]
    ends = jnp.cumsum(lengths[0])
    position = jnp.arange(rows, dtype=jnp.int32)
    doc_index = jnp.sum((position[:, None] >= ends[None, :]).astype(jnp.int32), axis=1)
    doc_hot = doc_index[:, None] == jnp.arange(DOCS, dtype=jnp.int32)[None, :]
    end_of = jnp.sum(jnp.where(doc_hot, ends[None, :], 0), axis=1)
    live = position + 1 != end_of
    domain = jnp.sum(jnp.where(doc_hot, doc_domain[0][None, :], 0), axis=1)
    onehot = (domain[:, None] == jnp.arange(DOMAINS, dtype=jnp.int32)[None, :]).astype(jnp.float32)
    selected = (live & (proxy_loss > reference_loss)).astype(jnp.float32)
    excess = selected * (proxy_loss - reference_loss)
    excess_part = jnp.sum(onehot * excess[:, None], axis=0)
    count_part = jnp.sum(onehot * live.astype(jnp.float32)[:, None], axis=0)
    return (onehot, selected, excess_part, count_part)


def domain_weights(statistics, log_weights, step_count, total_tokens):
    onehot, selected, excess_part, count_part = statistics
    excess_sum, count = lax.psum((excess_part, count_part), "dp")
    counts = jnp.maximum(count, 1.0)
    mean_excess = excess_sum / counts
    rate = 1.0 / jnp.sqrt(step_count[0].astype(jnp.float32))
    logits = log_weights + rate * mean_excess
    new_log = logits - jnp.log(jnp.sum(jnp.exp(logits)))
    lam = (1.0 - SMOOTH) * jnp.exp(new_log) + SMOOTH / DOMAINS
    per_domain = lam * total_tokens / counts
    weight = jnp.sum(onehot * per_domain[None, :], axis=1) * selected
    return (weight, new_log)


def local(
    section_inputs,
    gains,
    value_weight,
    top_cotangent,
    proxy_loss,
    reference_loss,
    lengths,
    doc_domain,
    log_weights,
    step_count,
):
    sections = lax.axis_size("section")
    section = lax.axis_index("section")
    devices = lax.axis_size("dp")
    xfull = section_inputs[0].astype(jnp.float32)
    gamma = gains[0]
    shard = value_weight[0]
    rows = xfull.shape[0]
    block = rows // MICRO
    total_tokens = rows * devices
    statistics = local_statistics(proxy_loss, reference_loss, lengths, doc_domain)
    weight, new_log = domain_weights(statistics, log_weights, step_count, total_tokens)
    inverse = lax.rsqrt(jnp.mean(xfull * xfull, axis=1, keepdims=True) + EPS)
    normed = (xfull * inverse * gamma[None, :]).astype(jnp.bfloat16)
    full_weight = lax.all_gather(shard, "dp", axis=0, tiled=True)
    act = jnp.dot(normed, full_weight, preferred_element_type=jnp.float32)
    hidden = jax.nn.silu(act).astype(jnp.bfloat16)
    kept_cot = jnp.zeros((rows, D), jnp.bfloat16)
    kept_da = jnp.zeros((rows, KV), jnp.float32)
    kept_dx = jnp.zeros((rows, D), jnp.bfloat16)
    state = (kept_cot, kept_da, kept_dx)
    received = jnp.zeros((block, D), jnp.bfloat16)
    ticks = MICRO + sections - 1
    for tick in range(ticks):
        index = tick - (sections - 1) + section
        active = (index >= 0) & (index < MICRO)
        start = jnp.clip(index, 0, MICRO - 1) * block
        top = lax.dynamic_slice_in_dim(top_cotangent, start, block, 0)
        incoming = jnp.where(section == sections - 1, top, received)

        def work(current):
            cot_buf, da_buf, dx_buf = current
            act_part = lax.dynamic_slice_in_dim(act, start, block, 0)
            x_part = lax.dynamic_slice_in_dim(xfull, start, block, 0)
            scale = lax.dynamic_slice_in_dim(inverse, start, block, 0)
            grad_h = jnp.einsum(
                "td,dk->tk", incoming, full_weight, preferred_element_type=jnp.float32
            )
            sig = jax.nn.sigmoid(act_part)
            grad_a = grad_h * sig * (1.0 + act_part * (1.0 - sig))
            grad_n = jnp.einsum(
                "tk,dk->td",
                grad_a.astype(jnp.bfloat16),
                full_weight,
                preferred_element_type=jnp.float32,
            )
            scaled = gamma[None, :] * grad_n
            grad_x = (
                incoming.astype(jnp.float32)
                + scale * scaled
                - x_part * scale**3 * jnp.mean(x_part * scaled, axis=1, keepdims=True)
            )
            passed = grad_x.astype(jnp.bfloat16)
            cot_buf = lax.dynamic_update_slice_in_dim(cot_buf, incoming, start, 0)
            da_buf = lax.dynamic_update_slice_in_dim(da_buf, grad_a, start, 0)
            dx_buf = lax.dynamic_update_slice_in_dim(dx_buf, passed, start, 0)
            return ((cot_buf, da_buf, dx_buf), passed)

        def skip(current):
            return (current, jnp.zeros((block, D), jnp.bfloat16))

        state, outgoing = lax.cond(active, work, skip, state)
        if tick + 1 < ticks:
            received = passed_along(outgoing, "section", -1)
    kept_cot, kept_da, kept_dx = state
    section_grad = (weight[:, None] * kept_dx.astype(jnp.float32)).astype(jnp.bfloat16)
    weighted_a = (weight[:, None] * kept_da).astype(jnp.bfloat16)
    weighted_g = (weight[:, None] * kept_cot.astype(jnp.float32)).astype(jnp.bfloat16)
    total = jnp.einsum("td,tk->dk", normed, weighted_a, preferred_element_type=jnp.float32)
    total = total + jnp.einsum("td,tk->dk", weighted_g, hidden, preferred_element_type=jnp.float32)
    grad_shard = lax.psum_scatter(total / devices, "dp", scatter_dimension=0, tiled=True)
    return (section_grad[None], grad_shard[None], new_log)


def solution(mesh):
    return jax.shard_map(
        local,
        mesh=mesh,
        in_specs=(
            P("section", "dp", None),
            P("section", None),
            P("section", "dp", None),
            P("dp", None),
            P("dp"),
            P("dp"),
            P("dp", None),
            P("dp", None),
            P(),
            P(),
        ),
        out_specs=(P("section", "dp", None), P("section", "dp", None), P()),
        check_vma=False,
    )
```

profile of v0, /device:TPU:0, one launch (start us, length us, event | category | flops | bytes accessed | tf_op | source)
XLA Modules:
  0.0 433.6 jit_solution(3129491005748980739)
XLA Ops:
  7.2 0.0 all-gather.3.cloned.1.call-start
  7.2 0.7 all-gather.3.cloned.1.call-update
  7.9 0.0 reduce-scatter.2.cloned.1.call-start
  8.0 1.5 multiply_reduce_fusion.7
  9.5 1.4 bitcast_convert_fusion
  10.9 83.5 %all-gather.3.cloned.1.call-done = bf16[1,4096,1024]{2,1,0:T(8,128)(2,1)} async-done(((bf16[1,512,1024]{2,1,0:T(8,128)(2,1)}), bf16[1,4096,1024]{2,1,0:T(8,128)(2,1)}) %all-gather.3.cloned.1.call-update) | async-done | bytes 8388624 | tf_op jit(solution)/shard_map/all_gather | solution.py:79
  94.4 5.0 %fusion.39 = f32[128,1024]{1,0:T(8,128)S(1)} fusion(bf16[1,128,4096]{2,1,0:T(8,128)(2,1)} %param.24, f32[4096]{0:T(1024)} %bitcast.103, f32[128]{0:T(128)S(1)} %get-tuple-element.1029, bf16[1,4096,1024]{2,1,0:T(8,128)(2,1)} %all-gather.3.cloned.1.call-done), kind=kOutput, calls=%fused_computation.121 | convolution fusion | flops 1075838976 | bytes 9978368 | tf_op jit(solution)/shard_map/dot_general | solution.py:80
  99.5 3.8 conditional.7
  99.5 0.8 broadcast.172
  100.3 0.8 broadcast_in_dim.22
  101.1 1.1 broadcast.171.clone
  102.2 1.1 broadcast.171
  103.3 1.3 collective-permute-start
  104.6 9.3 %collective-permute-done = bf16[32,4096]{1,0:T(8,128)(2,1)S(1)} collective-permute-done((bf16[32,4096]{1,0:T(8,128)(2,1)}, bf16[32,4096]{1,0:T(8,128)(2,1)S(1)}, u32[]{:S(2)}, u32[]{:S(2)}) %collective-permute-start) | collective-permute-done | bytes 262176 | tf_op jit(solution)/shard_map/ppermute | solution.py:20
  113.8 0.7 conditional.8
  113.8 0.7 broadcast.177
  114.6 1.3 collective-permute-start.1
  115.9 0.2 reduce-window.8
  116.1 0.1 convert_reduce_fusion
  116.2 8.8 %collective-permute-done.1 = bf16[32,4096]{1,0:T(8,128)(2,1)S(1)} collective-permute-done((bf16[32,4096]{1,0:T(8,128)(2,1)}, bf16[32,4096]{1,0:T(8,128)(2,1)S(1)}, u32[]{:S(2)}, u32[]{:S(2)}) %collective-permute-start.1) | collective-permute-done | bytes 262176 | tf_op jit(solution)/shard_map/ppermute | solution.py:20
  125.0 0.7 conditional.9
  125.0 0.7 broadcast.180
  125.7 1.3 collective-permute-start.2
  127.0 0.1 select_reduce_fusion.3
  127.8 37.2 %collective-permute-done.2 = bf16[32,4096]{1,0:T(8,128)(2,1)S(1)} collective-permute-done((bf16[32,4096]{1,0:T(8,128)(2,1)}, bf16[32,4096]{1,0:T(8,128)(2,1)S(1)}, u32[]{:S(2)}, u32[]{:S(2)}) %collective-permute-start.2) | collective-permute-done | bytes 262176 | tf_op jit(solution)/shard_map/ppermute | solution.py:20
  165.0 11.4 %conditional.10 = (bf16[128,4096]{1,0:T(8,128)(2,1)}, f32[128,1024]{1,0:T(8,128)}, bf16[128,4096]{1,0:T(8,128)(2,1)}, bf16[32,4096]{1,0:T(8,128)(2,1)}) conditional(s32[]{:T(128)} %convert_element_type.183, (bf16[128,4096]{1,0:T(8,128)(2,1)}, f32[128,1024]{1,0:T(8,128)}, bf16[128,4096]{1,0:T(8,128)(2,1)}) %tuple.114, (pred[]{:T(512)}, s32[]{:T(128)}, ...), branch_computations={%region_20.21_spmd, %region_21.23_spmd} | conditional | flops 538607680 | bytes 46548780 | solution.py:126
  165.0 1.9 constant_dynamic-update-slice_fusion.9
  166.9 5.8 %constant_dynamic-update-slice_fusion.8 = (f32[128,1024]{1,0:T(8,128)}, bf16[32,1024]{1,0:T(8,128)(2,1)S(1)}) fusion(f32[128,1024]{1,0:T(8,128)} %get-tuple-element.838, s32[]{:T(128)S(6)} %select_n.188, f32[128,1024]{1,0:T(8,128)S(1)} %get-tuple-element.840, bf16[32,4096]{1,0:T(8,128)(2,1)S(1)} %get-tuple-element.971, ...), kind=kOutput, calls=%fused_computation.56 | convolution fusion | flops 268730368 | bytes 8978436 | tf_op jit(solution)/shard_map/cond/branch_1_fun/td,dk->tk/dot_general | solution.py:100
  172.7 2.7 multiply_reduce_fusion.3
  175.4 0.1 fusion.19
  175.5 1.0 constant_dynamic-update-slice_fusion.10
  176.4 1.3 collective-permute-start.3
  177.7 0.1 select_reduce_fusion.1
  177.9 13.6 %all-reduce = (f32[22]{0:T(128)S(1)}, f32[22]{0:T(128)S(1)}) all-reduce(f32[22]{0:T(128)S(1)} %get-tuple-element.953, f32[22]{0:T(128)S(1)} %get-tuple-element.952), channel_id=1, replica_groups=mesh['section'=4,'dp'=8] {'dp'}, use_global_device_ids=true, to_apply=%region_5.6 | all-reduce | flops 44 | bytes 352 | tf_op jit(solution)/shard_map/psum | solution.py:42
  191.5 11.5 %conditional.11 = (bf16[128,4096]{1,0:T(8,128)(2,1)}, f32[128,1024]{1,0:T(8,128)}, bf16[128,4096]{1,0:T(8,128)(2,1)}, bf16[32,4096]{1,0:T(8,128)(2,1)}) conditional(s32[]{:T(128)} %convert_element_type.182, (bf16[128,4096]{1,0:T(8,128)(2,1)}, f32[128,1024]{1,0:T(8,128)}, bf16[128,4096]{1,0:T(8,128)(2,1)}) %tuple.116, (pred[]{:T(512)}, s32[]{:T(128)}, ...), branch_computations={%region_23.24_spmd, %region_24.26_spmd} | conditional | flops 538607680 | bytes 46548780 | solution.py:126
  191.5 1.9 constant_dynamic-update-slice_fusion.12
  193.4 5.8 %constant_dynamic-update-slice_fusion.11 = (f32[128,1024]{1,0:T(8,128)}, bf16[32,1024]{1,0:T(8,128)(2,1)S(1)}) fusion(f32[128,1024]{1,0:T(8,128)} %get-tuple-element.853, s32[]{:T(128)S(6)} %select_n.192, f32[128,1024]{1,0:T(8,128)S(1)} %get-tuple-element.855, bf16[32,4096]{1,0:T(8,128)(2,1)S(1)} %get-tuple-element.975, ...), kind=kOutput, calls=%fused_computation.71 | convolution fusion | flops 268730368 | bytes 8978436 | tf_op jit(solution)/shard_map/cond/branch_1_fun/td,dk->tk/dot_general | solution.py:100
  199.1 2.7 multiply_reduce_fusion.4
  201.9 0.1 fusion.23
  201.9 1.0 constant_dynamic-update-slice_fusion.13
  202.9 1.3 collective-permute-start.4
  204.2 0.6 exponential_reduce_fusion
  205.5 0.5 multiply_divide_fusion
  206.0 8.6 %collective-permute-done.4 = bf16[32,4096]{1,0:T(8,128)(2,1)S(1)} collective-permute-done((bf16[32,4096]{1,0:T(8,128)(2,1)}, bf16[32,4096]{1,0:T(8,128)(2,1)S(1)}, u32[]{:S(2)}, u32[]{:S(2)}) %collective-permute-start.4) | collective-permute-done | bytes 262176 | tf_op jit(solution)/shard_map/ppermute | solution.py:20
  214.6 11.3 %conditional.12 = (bf16[128,4096]{1,0:T(8,128)(2,1)}, f32[128,1024]{1,0:T(8,128)}, bf16[128,4096]{1,0:T(8,128)(2,1)}, bf16[32,4096]{1,0:T(8,128)(2,1)S(1)}) conditional(s32[]{:T(128)} %convert_element_type.181, (bf16[128,4096]{1,0:T(8,128)(2,1)}, f32[128,1024]{1,0:T(8,128)}, bf16[128,4096]{1,0:T(8,128)(2,1)}) %tuple.118, (pred[]{:T(512)}, ...), branch_computations={%region_26.27_spmd, %region_27.29_spmd} | conditional | flops 538607680 | bytes 46548780 | solution.py:126
  214.6 1.9 constant_dynamic-update-slice_fusion.15
  216.5 5.8 %constant_dynamic-update-slice_fusion.14 = (f32[128,1024]{1,0:T(8,128)}, bf16[32,1024]{1,0:T(8,128)(2,1)S(1)}) fusion(f32[128,1024]{1,0:T(8,128)} %get-tuple-element.868, s32[]{:T(128)S(6)} %select_n.196, f32[128,1024]{1,0:T(8,128)S(1)} %get-tuple-element.870, bf16[32,4096]{1,0:T(8,128)(2,1)S(1)} %get-tuple-element.979, ...), kind=kOutput, calls=%fused_computation.86 | convolution fusion | flops 268730368 | bytes 8978436 | tf_op jit(solution)/shard_map/cond/branch_1_fun/td,dk->tk/dot_general | solution.py:100
  222.3 2.7 multiply_reduce_fusion.5
  225.0 0.1 fusion.27
  225.1 0.9 constant_dynamic-update-slice_fusion.16
  226.0 0.7 copy-done.5
  226.7 1.3 collective-permute-start.5
  228.0 0.1 select_reduce_fusion
  228.1 9.5 %collective-permute-done.5 = bf16[32,4096]{1,0:T(8,128)(2,1)S(1)} collective-permute-done((bf16[32,4096]{1,0:T(8,128)(2,1)}, bf16[32,4096]{1,0:T(8,128)(2,1)S(1)}, u32[]{:S(2)}, u32[]{:S(2)}) %collective-permute-start.5) | collective-permute-done | bytes 262176 | tf_op jit(solution)/shard_map/ppermute | solution.py:20
  237.5 11.3 %conditional.13 = (f32[128,1024]{1,0:T(8,128)}, bf16[128,4096]{1,0:T(8,128)(2,1)}, bf16[128,4096]{1,0:T(8,128)(2,1)}) conditional(s32[]{:T(128)} %convert_element_type.180, (f32[128,1024]{1,0:T(8,128)}, bf16[128,4096]{1,0:T(8,128)(2,1)}, bf16[128,4096]{1,0:T(8,128)(2,1)}) %tuple.120, (pred[]{:T(512)}, s32[]{:T(128)}, bf16[128,4096]{1,0:T(8,128)(2,1)}, ...), branch_computations={%region_29.30_spmd, %region_30.32_spmd} | conditional | flops 538607680 | bytes 46286628 | solution.py:126
  237.5 0.1 fusion.32
  237.6 1.9 constant_dynamic-update-slice_fusion.17
  239.5 5.8 %constant_dynamic-update-slice_fusion.18 = (f32[128,1024]{1,0:T(8,128)}, bf16[32,1024]{1,0:T(8,128)(2,1)S(1)}) fusion(f32[128,1024]{1,0:T(8,128)} %get-tuple-element.875, s32[]{:T(128)S(6)} %select_n.200, f32[128,1024]{1,0:T(8,128)} %get-tuple-element.881, bf16[32,4096]{1,0:T(8,128)(2,1)S(1)} %get-tuple-element.981, bf16[4096,1024]{1,0:T(8,128)(2,1)} %get-tuple-element.880), kind=kOutput, calls=%fused_computation.103 | convolution fusion | flops 268730368 | bytes 8978436 | tf_op jit(solution)/shard_map/cond/branch_1_fun/td,dk->tk/dot_general | solution.py:100
  245.2 2.7 multiply_reduce_fusion.6
  247.9 0.9 fusion.29
  248.8 3.6 fusion.38
  252.4 9.5 %add_multiply_fusion = f32[4096,1024]{1,0:T(8,128)} fusion(f32[4096,1024]{1,0:T(8,128)S(1)} %fusion.38, bf16[128,4096]{1,0:T(8,128)(2,1)} %get-tuple-element.951, f32[128]{0:T(128)S(1)} %broadcast_select_fusion, f32[128,1024]{1,0:T(8,128)S(1)} %copy-done.2), kind=kOutput, calls=%fused_computation.108 | convolution fusion | flops 1084358656 | bytes 35127808 | tf_op jit(solution)/shard_map/td,tk->dk/dot_general | solution.py:134
  262.0 2.5 fusion.36
  264.4 162.3 %reduce-scatter.2.cloned.1.call-done = f32[512,1024]{1,0:T(8,128)} async-done(((f32[4096,1024]{1,0:T(8,128)}), f32[512,1024]{1,0:T(8,128)}) %reduce-scatter.2.cloned.1.call-update) | async-done | bytes 2097168 | tf_op jit(solution)/shard_map/reduce_scatter | solution.py:135
  (49 shorter events, 0.1 us)
Async XLA Ops:
  7.2 87.2 %all-gather.3.cloned.1.call-start = ((), (), s32[]{:S(2)}) async-start(), calls=%async_computation.2 | async-start | bytes 9437184 | tf_op jit(solution)/shard_map/all_gather | solution.py:79
  7.9 418.8 %reduce-scatter.2.cloned.1.call-start = ((), (), s32[]{:S(2)}) async-start(), calls=%async_computation.1 | async-start | bytes 18874368 | tf_op jit(solution)/shard_map/reduce_scatter | solution.py:135
  94.4 5.1 %copy-start.4 = (f32[1,4096]{1,0:T(1,128)S(1)}, f32[1,4096]{1,0:T(1,128)}, u32[]{:S(2)}) copy-start(f32[1,4096]{1,0:T(1,128)} %param.25) | copy-start | bytes 49156
  99.4 115.2 %copy-start.1 = (f32[128,1024]{1,0:T(8,128)}, f32[128,1024]{1,0:T(8,128)S(1)}, u32[]{:S(2)}) copy-start(f32[128,1024]{1,0:T(8,128)S(1)} %fusion.39) | copy-start | bytes 1572868
  103.3 10.6 %collective-permute-start = (bf16[32,4096]{1,0:T(8,128)(2,1)}, bf16[32,4096]{1,0:T(8,128)(2,1)S(1)}, u32[]{:S(2)}, u32[]{:S(2)}) collective-permute-start(bf16[32,4096]{1,0:T(8,128)(2,1)} %get-tuple-element.920), channel_id=1, source_target_pairs={{8,0},{16,8},{24,16},{9,1},{17,9},{25,17},{10,2},{18,10},{26,18},{... | collective-permute-start | bytes 786440 | tf_op jit(solution)/shard_map/ppermute | solution.py:20
  113.8 2.0 copy-start.10
  114.6 10.4 %collective-permute-start.1 = (bf16[32,4096]{1,0:T(8,128)(2,1)}, bf16[32,4096]{1,0:T(8,128)(2,1)S(1)}, u32[]{:S(2)}, u32[]{:S(2)}) collective-permute-start(bf16[32,4096]{1,0:T(8,128)(2,1)} %get-tuple-element.924), channel_id=1, source_target_pairs={{8,0},{16,8},{24,16},{9,1},{17,9},{25,17},{10,2},{18,10},{26,18},{... | collective-permute-start | bytes 786440 | tf_op jit(solution)/shard_map/ppermute | solution.py:20
  125.0 2.0 copy-start.8
  125.0 2.8 copy-start.6
  125.0 2.8 copy-start.7
  125.7 39.3 %collective-permute-start.2 = (bf16[32,4096]{1,0:T(8,128)(2,1)}, bf16[32,4096]{1,0:T(8,128)(2,1)S(1)}, u32[]{:S(2)}, u32[]{:S(2)}) collective-permute-start(bf16[32,4096]{1,0:T(8,128)(2,1)} %get-tuple-element.928), channel_id=1, source_target_pairs={{8,0},{16,8},{24,16},{9,1},{17,9},{25,17},{10,2},{18,10},{26,18},{... | collective-permute-start | bytes 786440 | tf_op jit(solution)/shard_map/ppermute | solution.py:20
  165.0 7.6 %slice-start.6 = ((s8[8388608]{0:T(1024)(128)(4,1)}), s8[4194304]{0:T(1024)(128)(4,1)S(1)}, s32[]{:S(2)}) async-start(s8[8388608]{0:T(1024)(128)(4,1)} %bitcast.95), calls=%async_computation.9 | async-start | bytes 8388608 | tf_op jit(solution)/shard_map/cond
  166.9 5.8 %slice-start.7 = ((s8[8388608]{0:T(1024)(128)(4,1)}), s8[4194304]{0:T(1024)(128)(4,1)S(1)}, s32[]{:S(2)}) async-start(s8[8388608]{0:T(1024)(128)(4,1)} %bitcast.95), calls=%async_computation.10 | async-start | bytes 8388608 | tf_op jit(solution)/shard_map/cond
  176.4 15.0 %collective-permute-start.3 = (bf16[32,4096]{1,0:T(8,128)(2,1)}, bf16[32,4096]{1,0:T(8,128)(2,1)S(1)}, u32[]{:S(2)}, u32[]{:S(2)}) collective-permute-start(bf16[32,4096]{1,0:T(8,128)(2,1)} %get-tuple-element.932), channel_id=1, source_target_pairs={{8,0},{16,8},{24,16},{9,1},{17,9},{25,17},{10,2},{18,10},{26,18},{... | collective-permute-start | bytes 786440 | tf_op jit(solution)/shard_map/ppermute | solution.py:20
  191.4 12.8 %copy-start.9 = (f32[22]{0:T(128)S(1)}, f32[22]{0:T(128)}, u32[]{:S(2)}) copy-start(f32[22]{0:T(128)} %param.32) | copy-start | bytes 268
  191.5 7.6 %slice-start.8 = ((s8[8388608]{0:T(1024)(128)(4,1)}), s8[4194304]{0:T(1024)(128)(4,1)S(1)}, s32[]{:S(2)}) async-start(s8[8388608]{0:T(1024)(128)(4,1)} %bitcast.97), calls=%async_computation.11 | async-start | bytes 8388608 | tf_op jit(solution)/shard_map/cond
  193.4 5.8 %slice-start.9 = ((s8[8388608]{0:T(1024)(128)(4,1)}), s8[4194304]{0:T(1024)(128)(4,1)S(1)}, s32[]{:S(2)}) async-start(s8[8388608]{0:T(1024)(128)(4,1)} %bitcast.97), calls=%async_computation.12 | async-start | bytes 8388608 | tf_op jit(solution)/shard_map/cond
  202.9 11.7 %collective-permute-start.4 = (bf16[32,4096]{1,0:T(8,128)(2,1)}, bf16[32,4096]{1,0:T(8,128)(2,1)S(1)}, u32[]{:S(2)}, u32[]{:S(2)}) collective-permute-start(bf16[32,4096]{1,0:T(8,128)(2,1)} %get-tuple-element.936), channel_id=1, source_target_pairs={{8,0},{16,8},{24,16},{9,1},{17,9},{25,17},{10,2},{18,10},{26,18},{... | collective-permute-start | bytes 786440 | tf_op jit(solution)/shard_map/ppermute | solution.py:20
  214.6 7.6 %slice-start.10 = ((s8[8388608]{0:T(1024)(128)(4,1)}), s8[4194304]{0:T(1024)(128)(4,1)S(1)}, s32[]{:S(2)}) async-start(s8[8388608]{0:T(1024)(128)(4,1)} %bitcast.99), calls=%async_computation.13 | async-start | bytes 8388608 | tf_op jit(solution)/shard_map/cond
  216.5 5.8 %slice-start.11 = ((s8[8388608]{0:T(1024)(128)(4,1)}), s8[4194304]{0:T(1024)(128)(4,1)S(1)}, s32[]{:S(2)}) async-start(s8[8388608]{0:T(1024)(128)(4,1)} %bitcast.99), calls=%async_computation.14 | async-start | bytes 8388608 | tf_op jit(solution)/shard_map/cond
  226.0 0.7 copy-start.5
  226.7 10.8 %collective-permute-start.5 = (bf16[32,4096]{1,0:T(8,128)(2,1)}, bf16[32,4096]{1,0:T(8,128)(2,1)S(1)}, u32[]{:S(2)}, u32[]{:S(2)}) collective-permute-start(bf16[32,4096]{1,0:T(8,128)(2,1)} %copy-done.5), channel_id=1, source_target_pairs={{8,0},{16,8},{24,16},{9,1},{17,9},{25,17},{10,2},{18,10},{26,18},{... | collective-permute-start | bytes 786440 | tf_op jit(solution)/shard_map/ppermute | solution.py:20
  237.5 11.3 %copy-start = (bf16[1,128,4096]{2,1,0:T(8,128)(2,1)S(1)}, bf16[1,128,4096]{2,1,0:T(8,128)(2,1)}, u32[]{:S(2)}) copy-start(bf16[1,128,4096]{2,1,0:T(8,128)(2,1)} %param.24) | copy-start | bytes 3145732
  237.6 7.6 %slice-start.12 = ((s8[8388608]{0:T(1024)(128)(4,1)}), s8[4194304]{0:T(1024)(128)(4,1)S(1)}, s32[]{:S(2)}) async-start(s8[8388608]{0:T(1024)(128)(4,1)} %bitcast.101), calls=%async_computation.15 | async-start | bytes 8388608 | tf_op jit(solution)/shard_map/cond
  239.5 5.8 %slice-start.13 = ((s8[8388608]{0:T(1024)(128)(4,1)}), s8[4194304]{0:T(1024)(128)(4,1)S(1)}, s32[]{:S(2)}) async-start(s8[8388608]{0:T(1024)(128)(4,1)} %bitcast.101), calls=%async_computation.16 | async-start | bytes 8388608 | tf_op jit(solution)/shard_map/cond
  248.8 3.6 copy-start.2
Sparse Core Ops, SparseCore 0:
  9.6 84.7 all-gather.2
  262.1 164.5 reduce-scatter.1
where the time goes:
time: 434 us
  waiting for transfers between devices  320 us (74%)
  matrix products  52 us (12%)
  other arithmetic  18.7 us (4%)
  between operations  15.6 us (4%)
  blocking collectives  13.6 us (3%)
  starting transfers between devices  7.76 us (2%)
  local copies, waits for them, and re-layouts  6.04 us (1%)
    reduce_scatter x1, waiting for transfers between devices, local(): lax.psum_scatter(total / devices, 'dp', scatter_dimension=0, tiled=True)  162 us
    all_gather x1, waiting for transfers between devices, local(): full_weight = lax.all_gather(shard, 'dp', axis=0, tiled=True)  83.5 us
    ppermute x6, waiting for transfers between devices, passed_along(): return lax.ppermute(shard, axis, pairs)  73.3 us
    dot_general x4, matrix products, work(): jnp.einsum('td,dk->tk', incoming, full_weight, preferred_element_type=jnp...  23 us
    psum x1, blocking collectives, domain_weights(): excess_sum, count = lax.psum((excess_part, count_part), 'dp')  13.6 us
    dot_general x4, matrix products, work(): jnp.einsum('tk,dk->td', grad_a.astype(jnp.bfloat16), full_weight, preferr...  10.9 us
    dot_general x1, matrix products, local(): jnp.einsum('td,tk->dk', weighted_g, hidden, preferred_element_type=jnp.fl...  9.51 us
  transfers between devices with their start and end apart: 8, of which 7 were waited for; matrix products, arithmetic and copies ran while one was open for 2% of the time, Pallas kernels for 0%

commit v1 on v0

--- a/solution.py
+++ b/solution.py
@@ -1,12 +1,18 @@
+import functools
+
 import jax
 import jax.numpy as jnp
 from jax import lax
+from jax.experimental import pallas as pl
+from jax.experimental.pallas import tpu as pltpu
 from jax.sharding import PartitionSpec as P
 
 D = 4096
 KV = 1024
 DOMAINS = 22
 MICRO = 4
+LANES = 128
+MESH = pl.DeviceIdType.MESH
 DOCS = 8
 
 
@@ -136,9 +142,499 @@
     return (section_grad[None], grad_shard[None], new_log)
 
 
+def relay_kernel(
+    devices,
+    sections,
+    x_ref,
+    gamma_ref,
+    shard_ref,
+    top_ref,
+    stat_ref,
+    onehot_ref,
+    selected_ref,
+    logw_ref,
+    rate_ref,
+    sg_ref,
+    wg_ref,
+    log_ref,
+    w_full,
+    normed,
+    cot,
+    passed,
+    w_cot,
+    act,
+    dh,
+    scaled,
+    inverse,
+    weight,
+    stats,
+    hid_full,
+    da_full,
+    n_col,
+    g_col,
+    n_colt,
+    g_colt,
+    w_send,
+    w_recv,
+    s_send,
+    s_recv,
+    n_send,
+    n_recv,
+    h_send,
+    h_recv,
+    g_send,
+    g_recv,
+    a_send,
+    a_recv,
+    f_send,
+    f_recv,
+    r_send,
+    r_recv,
+):
+    rows, width = x_ref.shape
+    depth, kv = shard_ref.shape
+    block = rows // MICRO
+    chips = devices // 2
+    section = lax.axis_index("section")
+    me = lax.axis_index("dp")
+    chip, core = me // 2, me % 2
+    sibling = chip * 2 + (1 - core)
+
+    def tile(i, size):
+        return pl.ds(pl.multiple_of(i * size, size), size)
+
+    def remote(src, dst, send, recv, **where):
+        return pltpu.make_async_remote_copy(
+            src_ref=src, dst_ref=dst, send_sem=send, recv_sem=recv, device_id=where, device_id_type=MESH
+        )
+
+    def other(k):
+        return lax.rem(me + k, devices)
+
+    def peer(k):
+        return lax.rem(chip + k, chips) * 2 + core
+
+    barrier = pltpu.get_barrier_semaphore()
+    for k in range(1, devices):
+        pl.semaphore_signal(barrier, inc=1, device_id={"dp": other(k)}, device_id_type=MESH)
+    for k in (1, sections - 1):
+        pl.semaphore_signal(
+            barrier, inc=1, device_id={"section": lax.rem(section + k, sections)}, device_id_type=MESH
+        )
+    pl.semaphore_wait(barrier, devices + 1)
+
+    def w_own(kind, where):
+        return remote(shard_ref, w_full.at[tile(me, depth)], w_send.at[kind, me], w_recv.at[me], dp=where)
+
+    def w_copy(kind, j, where):
+        view = w_full.at[tile(j, depth)]
+        return remote(view, view, w_send.at[kind, j], w_recv.at[j], dp=where)
+
+    up, down = me + 2, me - 2
+
+    @pl.when(chip + 1 < chips)
+    def _():
+        w_own(0, up).start()
+
+    @pl.when(chip > 0)
+    def _():
+        w_own(1, down).start()
+
+    w_own(2, sibling).start()
+
+    def s_copy(k):
+        return remote(stat_ref, stats.at[me], s_send.at[k], s_recv.at[me], dp=other(k))
+
+    for k in range(1, devices):
+        s_copy(k).start()
+    stats[me] = stat_ref[...]
+    w_full[tile(me, depth), :] = shard_ref[...]
+
+    square = jnp.zeros((rows, 1), jnp.float32)
+    for j in range(devices):
+        xs = x_ref[:, j * depth : (j + 1) * depth].astype(jnp.float32)
+        square = square + jnp.sum(xs * xs, axis=1, keepdims=True)
+    inverse[...] = lax.rsqrt(square / width + EPS)
+
+    @pl.loop(0, devices)
+    def _(j):
+        xs = x_ref[:, tile(j, depth)].astype(jnp.float32)
+        normed[:, tile(j, depth)] = (xs * inverse[...] * gamma_ref[:, tile(j, depth)]).astype(jnp.bfloat16)
+
+    is_top = section == sections - 1
+
+    @pl.when(is_top)
+    def _():
+        cot[...] = top_ref[...]
+
+    act[...] = jnp.zeros_like(act)
+    dh[...] = jnp.zeros_like(dh)
+
+    def absorb(j):
+        act[...] += jnp.dot(normed[:, tile(j, depth)], w_full[tile(j, depth), :], preferred_element_type=jnp.float32)
+
+        @pl.when(is_top)
+        def _():
+            dh[...] += jnp.dot(cot[:, tile(j, depth)], w_full[tile(j, depth), :], preferred_element_type=jnp.float32)
+
+    absorb(me)
+    w_copy(2, sibling, sibling).wait_recv()
+    absorb(sibling)
+
+    for k in range(1, devices):
+        j = other(k)
+        remote(stats.at[j], stats.at[j], s_send.at[k], s_recv.at[j], dp=sibling).wait_recv()
+    total = stats[0]
+    for j in range(1, devices):
+        total = total + stats[j]
+    counts = jnp.maximum(total[1:2], 1.0)
+    logits = logw_ref[...] + rate_ref[...] * (total[0:1] / counts)
+    valid = lax.broadcasted_iota(jnp.int32, logits.shape, 1) < DOMAINS
+    new_log = logits - jnp.log(jnp.sum(jnp.where(valid, jnp.exp(logits), 0.0), axis=1, keepdims=True))
+    log_ref[...] = new_log
+    lam = (1.0 - SMOOTH) * jnp.exp(new_log) + SMOOTH / DOMAINS
+    per_domain = lam * (rows * devices) / counts
+    weight[...] = jnp.sum(onehot_ref[...] * per_domain, axis=1, keepdims=True) * selected_ref[...]
+
+    for hop in range(1, chips):
+        below, above = me - 2 * hop, me + 2 * hop
+
+        @pl.when(chip >= hop)
+        def _():
+            w_copy(0, below, sibling).wait_recv()
+
+            @pl.when(chip + 1 < chips)
+            def _():
+                w_copy(0, below, up).start()
+
+            w_copy(2, below, sibling).start()
+
+        @pl.when(chip + hop < chips)
+        def _():
+            w_copy(1, above, sibling).wait_recv()
+
+            @pl.when(chip > 0)
+            def _():
+                w_copy(1, above, down).start()
+
+            w_copy(2, above, sibling).start()
+
+        @pl.when(chip >= hop)
+        def _():
+            absorb(below)
+            j = sibling - 2 * hop
+            w_copy(2, j, sibling).wait_recv()
+            absorb(j)
+
+        @pl.when(chip + hop < chips)
+        def _():
+            absorb(above)
+            j = sibling + 2 * hop
+            w_copy(2, j, sibling).wait_recv()
+            absorb(j)
+
+    def n_copy(k):
+        j = other(k)
+        return remote(
+            normed.at[:, tile(j, depth)], n_col.at[tile(me, rows)], n_send.at[k], n_recv.at[me], dp=j
+        )
+
+    a = act[...]
+    hid_full[tile(me, rows), :] = (a * jax.nn.sigmoid(a)).astype(jnp.bfloat16)
+    n_col[tile(me, rows), :] = normed[:, tile(me, depth)]
+
+    def h_copy(k):
+        view = hid_full.at[tile(me, rows)]
+        return remote(view, view, h_send.at[k], h_recv.at[me], dp=sibling if k == 0 else peer(k))
+
+    for k in range(1, devices):
+        n_copy(k).start()
+    for k in range(chips):
+        h_copy(k).start()
+
+    def r_copy(m):
+        return remote(
+            passed.at[tile(m, block)], cot.at[tile(m, block)], r_send.at[m], r_recv.at[m], section=section - 1
+        )
+
+    def g_copy(k, m):
+        j = other(k)
+        return remote(
+            w_cot.at[tile(m, block), tile(j, depth)],
+            g_col.at[tile(me * MICRO + m, block)],
+            g_send.at[k, m],
+            g_recv.at[me, m],
+            dp=j,
+        )
+
+    def a_copy(k, m):
+        view = da_full.at[tile(me * MICRO + m, block)]
+        return remote(view, view, a_send.at[k, m], a_recv.at[me, m], dp=sibling if k == 0 else peer(k))
+
+    @pl.loop(0, MICRO)
+    def _(m):
+        part = tile(m, block)
+
+        @pl.when(section < sections - 1)
+        def _():
+            r_copy(m).wait_recv()
+
+            @pl.loop(0, kv // 256)
+            def _(n):
+                dh[part, tile(n, 256)] = jnp.dot(
+                    cot[part, :], w_full[:, tile(n, 256)], preferred_element_type=jnp.float32
+                )
+
+        a = act[part, :]
+        sig = jax.nn.sigmoid(a)
+        grad_a = dh[part, :] * sig * (1.0 + a * (1.0 - sig))
+        da_full[tile(me * MICRO + m, block), :] = (weight[part, :] * grad_a).astype(jnp.bfloat16)
+        low = grad_a.astype(jnp.bfloat16)
+
+        def back(j, sums):
+            grad_n = lax.dot_general(
+                low,
+                w_full[tile(j, depth), :],
+                (((1,), (1,)), ((), ())),
+                preferred_element_type=jnp.float32,
+            )
+            u = gamma_ref[:, tile(j, depth)] * grad_n
+            scaled[:, tile(j, depth)] = u
+            xs = x_ref[part, tile(j, depth)].astype(jnp.float32)
+            return sums + jnp.sum(xs * u, axis=1, keepdims=True)
+
+        sums = lax.fori_loop(0, devices, back, jnp.zeros((block, 1), jnp.float32))
+        r = inverse[part, :]
+        cube = r * r * r * (sums / width)
+
+        @pl.loop(0, devices)
+        def _(j):
+            cols = tile(j, depth)
+            xs = x_ref[part, cols].astype(jnp.float32)
+            g = cot[part, cols].astype(jnp.float32)
+            passed[part, cols] = (g + r * scaled[:, cols] - xs * cube).astype(jnp.bfloat16)
+
+        @pl.when(section > 0)
+        def _():
+            r_copy(m).start()
+
+        for k in range(chips):
+            a_copy(k, m).start()
+
+        @pl.loop(0, devices)
+        def _(j):
+            cols = tile(j, depth)
+            w = weight[part, :]
+            w_cot[part, cols] = (w * cot[part, cols].astype(jnp.float32)).astype(jnp.bfloat16)
+            sg_ref[part, cols] = (w * passed[part, cols].astype(jnp.float32)).astype(jnp.bfloat16)
+
+        for k in range(1, devices):
+            g_copy(k, m).start()
+        g_col[tile(me * MICRO + m, block), :] = w_cot[part, tile(me, depth)]
+
+    def f_copy(kind, buf, k, src):
+        view = buf.at[tile(src, rows)]
+        return remote(view, view, f_send.at[kind, k], f_recv.at[kind, k], dp=sibling)
+
+    def h_arrived(j):
+        view = hid_full.at[tile(j, rows)]
+        remote(view, view, h_send.at[0], h_recv.at[j], dp=sibling).wait_recv()
+
+    def a_arrived(j):
+        for m in range(MICRO):
+            view = da_full.at[tile(j * MICRO + m, block)]
+            remote(view, view, a_send.at[0, m], a_recv.at[j, m], dp=sibling).wait_recv()
+
+    for k in range(1, chips):
+        h_arrived(peer(k))
+        f_copy(0, hid_full, k, peer(k)).start()
+    for k in range(1, devices):
+        j = other(k)
+        view = n_col.at[tile(j, rows)]
+        remote(view, view, n_send.at[k], n_recv.at[j], dp=sibling).wait_recv()
+
+    @pl.loop(0, devices)
+    def _(j):
+        n_colt[:, tile(j, rows)] = n_col[tile(j, rows), :].T
+
+    for k in range(1, chips):
+        a_arrived(peer(k))
+        f_copy(1, da_full, k, peer(k)).start()
+    h_arrived(sibling)
+    a_arrived(sibling)
+
+    for k in range(1, devices):
+        j = other(k)
+        for m in range(MICRO):
+            view = g_col.at[tile(j * MICRO + m, block)]
+            remote(view, view, g_send.at[k, m], g_recv.at[j, m], dp=sibling).wait_recv()
+
+    @pl.loop(0, devices)
+    def _(j):
+        g_colt[:, tile(j, rows)] = g_col[tile(j, rows), :].T
+
+    for k in range(1, chips):
+        far = lax.rem(chip + k, chips) * 2 + (1 - core)
+        f_copy(0, hid_full, k, far).wait_recv()
+        f_copy(1, da_full, k, far).wait_recv()
+
+    @pl.loop(0, kv // 256)
+    def _(n):
+        cols = tile(n, 256)
+        grad = jnp.dot(n_colt[...], da_full[:, cols], preferred_element_type=jnp.float32)
+        grad = grad + jnp.dot(g_colt[...], hid_full[:, cols], preferred_element_type=jnp.float32)
+        wg_ref[:, cols] = grad / devices
+
+    for k in range(1, devices):
+        s_copy(k).wait_send()
+        n_copy(k).wait_send()
+        for m in range(MICRO):
+            g_copy(k, m).wait_send()
+    for k in range(chips):
+        h_copy(k).wait_send()
+        for m in range(MICRO):
+            a_copy(k, m).wait_send()
+    for k in range(1, chips):
+        f_copy(0, hid_full, k, peer(k)).wait_send()
+        f_copy(1, da_full, k, peer(k)).wait_send()
+
+    @pl.when(section > 0)
+    def _():
+        for m in range(MICRO):
+            r_copy(m).wait_send()
+
+    @pl.when(chip + 1 < chips)
+    def _():
+        w_own(0, up).wait_send()
+
+    @pl.when(chip > 0)
+    def _():
+        w_own(1, down).wait_send()
+
+    w_own(2, sibling).wait_send()
+    for hop in range(1, chips):
+        below, above = me - 2 * hop, me + 2 * hop
+
+        @pl.when(chip >= hop)
+        def _():
+            @pl.when(chip + 1 < chips)
+            def _():
+                w_copy(0, below, up).wait_send()
+
+            w_copy(2, below, sibling).wait_send()
+
+        @pl.when(chip + hop < chips)
+        def _():
+            @pl.when(chip > 0)
+            def _():
+                w_copy(1, above, down).wait_send()
+
+            w_copy(2, above, sibling).wait_send()
+
+
+def fused(
+    section_inputs,
+    gains,
+    value_weight,
+    top_cotangent,
+    proxy_loss,
+    reference_loss,
+    lengths,
+    doc_domain,
+    log_weights,
+    step_count,
+):
+    devices = lax.axis_size("dp")
+    sections = lax.axis_size("section")
+    rows, width = top_cotangent.shape
+    depth, kv = value_weight.shape[1:]
+    onehot, selected, excess_part, count_part = local_statistics(
+        proxy_loss, reference_loss, lengths, doc_domain
+    )
+    spare = LANES - DOMAINS
+    stat = jnp.pad(jnp.stack([excess_part, count_part]), ((0, 6), (0, spare)))
+    rate = 1.0 / jnp.sqrt(step_count.astype(jnp.float32))
+    bf, f32 = jnp.bfloat16, jnp.float32
+    chips = devices // 2
+    dma = pltpu.SemaphoreType.DMA
+    flops = 2 * rows * width * kv * 5
+    vmem = pl.BlockSpec(memory_space=pltpu.VMEM)
+    section_grad, grad_shard, new_log = pl.pallas_call(
+        functools.partial(relay_kernel, devices, sections),
+        out_shape=(
+            jax.ShapeDtypeStruct((rows, width), bf),
+            jax.ShapeDtypeStruct((depth, kv), f32),
+            jax.ShapeDtypeStruct((1, LANES), f32),
+        ),
+        in_specs=[vmem] * 9,
+        out_specs=(vmem,) * 3,
+        scratch_shapes=[
+            pltpu.VMEM((width, kv), bf),
+            pltpu.VMEM((rows, width), bf),
+            pltpu.VMEM((rows, width), bf),
+            pltpu.VMEM((rows, width), bf),
+            pltpu.VMEM((rows, width), bf),
+            pltpu.VMEM((rows, kv), f32),
+            pltpu.VMEM((rows, kv), f32),
+            pltpu.VMEM((rows // MICRO, width), f32),
+            pltpu.VMEM((rows, 1), f32),
+            pltpu.VMEM((rows, 1), f32),
+            pltpu.VMEM((devices, 8, LANES), f32),
+            pltpu.VMEM((rows * devices, kv), bf),
+            pltpu.VMEM((rows * devices, kv), bf),
+            pltpu.VMEM((rows * devices, depth), bf),
+            pltpu.VMEM((rows * devices, depth), bf),
+            pltpu.VMEM((depth, rows * devices), bf),
+            pltpu.VMEM((depth, rows * devices), bf),
+            dma((3, devices)),
+            dma((devices,)),
+            dma((devices,)),
+            dma((devices,)),
+            dma((devices,)),
+            dma((devices,)),
+            dma((chips,)),
+            dma((devices,)),
+            dma((devices, MICRO)),
+            dma((devices, MICRO)),
+            dma((chips, MICRO)),
+            dma((devices, MICRO)),
+            dma((2, chips)),
+            dma((2, chips)),
+            dma((MICRO,)),
+            dma((MICRO,)),
+        ],
+        compiler_params=pltpu.CompilerParams(
+            collective_id=0, has_side_effects=True, vmem_limit_bytes=50 * 2**20
+        ),
+        cost_estimate=pl.CostEstimate(
+            flops=flops, bytes_accessed=2 * width * kv, transcendentals=rows * kv
+        ),
+    )(
+        section_inputs[0],
+        gains,
+        value_weight[0],
+        top_cotangent,
+        stat,
+        jnp.pad(onehot, ((0, 0), (0, spare))),
+        selected[:, None],
+        jnp.pad(log_weights, (0, spare))[None],
+        jnp.broadcast_to(rate[:, None], (1, LANES)),
+    )
+    return (section_grad[None], grad_shard[None], new_log[0, :DOMAINS])
+
+
+def choose(*args):
+    depth, kv = args[2].shape[1:]
+    devices = lax.axis_size("dp")
+    held = 2 * kv * (depth * devices + 2 * args[3].shape[0] * devices)
+    if devices % 2 == 0 and depth % LANES == 0 and held <= 2**24:
+        return fused(*args)
+    return local(*args)
+
+
 def solution(mesh):
     return jax.shard_map(
-        local,
+        choose,
         mesh=mesh,
         in_specs=(
             P("section", "dp", None),

time: 434 us -> 204 us (0.47)
  waiting for transfers between devices: 320 us -> 0 us
  Pallas kernels: 0 us -> 189 us
  matrix products: 52 us -> 0 us
  other arithmetic: 18.7 us -> 3.24 us
  between operations: 15.6 us -> 1.38 us
  blocking collectives: 13.6 us -> 0 us
  starting transfers between devices: 7.76 us -> 0 us
    pallas_call x0 -> x1, Pallas kernels: none -> 189 us  [fused(): pl.pallas_call(functools.partial(relay_kernel, devices, sections), out_sh...]
    reduce_scatter x1 -> x0, waiting for transfers between devices: 162 us -> none  [local(): lax.psum_scatter(total / devices, 'dp', scatter_dimension=0, tiled=True)]
    all_gather x1 -> x0, waiting for transfers between devices: 83.5 us -> none  [local(): full_weight = lax.all_gather(shard, 'dp', axis=0, tiled=True)]
    ppermute x6 -> x0, waiting for transfers between devices: 73.3 us -> none  [passed_along(): return lax.ppermute(shard, axis, pairs)]
    dot_general x11 -> x0, matrix products: 52 us -> none  [the longest x4 23 us: work(): jnp.einsum('td,dk->tk', incoming, full_weight, preferred_element_type=jnp...]
    psum x1 -> x0, blocking collectives: 13.6 us -> none  [domain_weights(): excess_sum, count = lax.psum((excess_part, count_part), 'dp')]
    dynamic_update_slice x8 -> x0, other arithmetic: 11.2 us -> none  [the longest x4 7.46 us: work(): cot_buf = lax.dynamic_update_slice_in_dim(cot_buf, incoming, start, 0)]
    ppermute x6 -> x0, starting transfers between devices: 7.68 us -> none  [passed_along(): return lax.ppermute(shard, axis, pairs)]
  transfers between devices with their start and end apart: 8 -> 0, of which waited for: 7 -> 0; matrix products, arithmetic and copies ran while one was open for 2% -> 0% of each run, Pallas kernels for 0% -> 0%
where the time goes in v1:
time: 204 us; the launch traced here: 201 us
  Pallas kernels  189 us (93%)
  local copies, waits for them, and re-layouts  7.08 us (3%)
  other arithmetic  3.24 us (2%)
    pallas_call x1, Pallas kernels, fused(): pl.pallas_call(functools.partial(relay_kernel, devices, sections), out_sh...  189 us
    unnamed x10, local copies, waits for them, and re-layouts  5.79 us

profile of v1, /device:TPU:0, one launch (start us, length us, event | category | flops | bytes accessed | tf_op | source)
XLA Modules:
  0.0 200.9 jit_solution(9181129405808198767)
XLA Ops:
  1.3 0.8 reduce-window.8
  2.2 0.1 convert_reduce_fusion
  2.2 0.7 select_reduce_fusion.3
  3.0 0.7 subtract_select_fusion
  3.7 0.7 pad_bitcast_fusion.logw_ref
  4.3 0.7 convert_bitcast_fusion
  5.0 0.1 select_reduce_fusion.1
  5.1 0.1 iota_compare_fusion
  5.3 0.1 copy.14.selected_ref
  5.4 0.0 copy-start
  5.4 1.2 copy-done
  6.6 0.0 copy-start.1
  6.6 1.2 copy-done.1
  7.8 0.0 copy-start.2
  7.8 0.7 copy-done.2
  8.5 189.2 %shard_map.121 = (bf16[128,4096]{1,0:T(8,128)(2,1)S(1)}, f32[512,1024]{1,0:T(8,128)}, f32[1,128]{1,0:T(1,128)S(1)}) custom-call(bf16[128,4096]{1,0:T(8,128)(2,1)S(1)} %bitcast.17, f32[1,4096]{1,0:T(1,128)S(1)} %copy-done.2, bf16[512,1024]{1,0:T(8,128)(2,1)S(1)} %bitcast.18, bf16[128,4096]{1,0:T(8,128)(2,1)} %top_ref.1, ...), custom_call_target="tpu_custom_call" | custom-call | flops 5368709120 | bytes 8388608 | tf_op jit(solution)/shard_map/pallas_call | solution.py:562
  197.8 0.0 copy-start.3
  197.8 0.5 slice_bitcast_fusion
  198.3 1.0 copy.18
  199.3 0.3 copy-done.3
  199.6 1.3 copy.19
  (3 shorter events, 0.0 us)
Async XLA Ops:
  5.4 1.2 copy-start
  6.6 1.2 copy-start.1
  7.8 0.7 copy-start.2
  197.8 1.8 copy-start.3
